TPU v7x, 32 devices: a whole 2x2x4 slice. The times are simulated.
32 devices in a mesh: section: 16 (over z, y, core), dp: 2 (over x).
Axes of the slice: x: 2, y: 2, z: 4, core: 2. Of those that a mesh axis runs over, the one named last changes fastest.
Arguments:
- fwd_h: bfloat16 [16, 256, 2048], P('section', None, 'dp'), may hold values from -6 to 6
- fwd_mem: bfloat16 [16, 256, 2048], P('section', None, 'dp'), may hold values from -6 to 6
- saved_h: bfloat16 [16, 256, 2048], P('section', None, 'dp'), may hold values from -6 to 6
- saved_mem: bfloat16 [16, 256, 2048], P('section', None, 'dp'), may hold values from -6 to 6
- back_h: bfloat16 [16, 256, 2048], P('section', None, 'dp'), may hold values from -6 to 6
- back_mem: bfloat16 [16, 256, 2048], P('section', None, 'dp'), may hold values from -6 to 6
- weight: bfloat16 [16, 2048, 2048], P('section', None, 'dp'), may hold values from -0.125 to 0.125
- row_stat: float32 [16, 2048], P('section'), may hold values from 0.05 to 5
- col_stat: float32 [16, 2048], P('section', 'dp'), may hold values from 0.05 to 5
- enc_count: int32 [1], replicated, may hold values from 4 to 12
- target_embed: bfloat16 [256, 2048], P(None, 'dp'), may hold values from -6 to 6
Outputs:
- next_h: bfloat16 [16, 256, 2048], P('section', None, 'dp')
- next_mem: bfloat16 [16, 256, 2048], P('section', None, 'dp')
- prev_h: bfloat16 [16, 256, 2048], P('section', None, 'dp')
- prev_mem: bfloat16 [16, 256, 2048], P('section', None, 'dp')
- update: bfloat16 [16, 2048, 2048], P('section', None, 'dp')
- row_new: float32 [16, 2048], P('section')
- col_new: float32 [16, 2048], P('section', 'dp')
Inputs may be any that keep to these rules, and one draw needn't show every extreme that they name: Sections 0 to enc_count - 1 are encoder sections, the others decoder sections.
All inputs are finite; a program needn't handle non-finite values.
Results may differ from a plain program's by a relative error of at most 0.0086.
Values may be sent and summed in bfloat16 or wider, within the bound.
A program may use at most 128 MiB of HBM per device.

v0:
```python
import jax
import jax.numpy as jnp
from jax import lax
from jax.sharding import PartitionSpec as P

HD = 256


EPS = 1e-06
BETA = 0.8
TINY = 1e-30


def from_behind(x, axis, by):
    devices = lax.axis_size(axis)
    pairs = [(i, i + by) for i in range(devices) if 0 <= i + by < devices]
    return lax.ppermute(x, axis, pairs)


def normalize(values):
    inv = lax.rsqrt(jnp.mean(values * values, axis=-1, keepdims=True) + EPS)
    return (values * inv, inv)


def inner_rows(left, right):
    return lax.dot_general(
        left, right, (((0,), (0,)), ((), ())), preferred_element_type=jnp.float32
    )


def outer_cols(left, right):
    return lax.dot_general(
        left, right, (((1,), (1,)), ((), ())), preferred_element_type=jnp.float32
    )


def attend(hn, cn, weight):
    scale = 1.0 / HD**0.5
    rows = hn.shape[0]
    heads = weight.shape[1] // HD
    queries = jnp.dot(hn, weight, preferred_element_type=jnp.float32).astype(jnp.bfloat16)
    keyvals = jnp.dot(cn, weight, preferred_element_type=jnp.float32).astype(jnp.bfloat16)
    q3 = queries.reshape(rows, heads, HD)
    kv3 = keyvals.reshape(rows, heads, HD)
    scores = jnp.einsum("qhd,khd->hqk", q3, kv3, preferred_element_type=jnp.float32) * scale
    probs = jax.nn.softmax(scores, axis=-1)
    probs_b = probs.astype(jnp.bfloat16)
    mixed = jnp.einsum("hqk,khd->qhd", probs_b, kv3, preferred_element_type=jnp.float32)
    return (q3, kv3, probs, probs_b, mixed.astype(jnp.bfloat16).reshape(rows, heads * HD))


def attend_back(q3, kv3, probs, probs_b, dmix):
    scale = 1.0 / HD**0.5
    rows, heads = (q3.shape[0], q3.shape[1])
    d3 = dmix.reshape(rows, heads, HD)
    dprobs = jnp.einsum("qhd,khd->hqk", d3, kv3, preferred_element_type=jnp.float32)
    dval = jnp.einsum("hqk,qhd->khd", probs_b, d3, preferred_element_type=jnp.float32)
    dscore = (probs * (dprobs - jnp.sum(dprobs * probs, axis=-1, keepdims=True)) * scale).astype(
        jnp.bfloat16
    )
    dq = jnp.einsum("hqk,khd->qhd", dscore, kv3, preferred_element_type=jnp.float32).astype(
        jnp.bfloat16
    )
    dk = jnp.einsum("hqk,qhd->khd", dscore, q3, preferred_element_type=jnp.float32)
    dkv = (dk + dval).astype(jnp.bfloat16)
    return (dq.reshape(rows, heads * HD), dkv.reshape(rows, heads * HD))


def on_device(
    fwd_h,
    fwd_mem,
    saved_h,
    saved_mem,
    back_h,
    back_mem,
    weight,
    row_stat,
    col_stat,
    enc_count,
    target_embed,
):
    section = lax.axis_index("section")
    first_dec = enc_count[0]
    decoder = section >= first_dec
    dec_flag = decoder.astype(jnp.float32)
    proj = weight[0]
    local_width = fwd_h.shape[2]
    start = lax.axis_index("dp") * local_width
    inputs = jnp.where(section == first_dec, target_embed, fwd_h[0])
    context = jnp.where(decoder, fwd_mem[0], inputs)
    full_h, full_c = (
        lax.all_gather(inputs, "dp", axis=1, tiled=True),
        lax.all_gather(context, "dp", axis=1, tiled=True),
    )
    hn_f, unused_h = normalize(full_h.astype(jnp.float32))
    cn_f, unused_c = normalize(full_c.astype(jnp.float32))
    parts = attend(hn_f.astype(jnp.bfloat16), cn_f.astype(jnp.bfloat16), proj)
    partial_value = outer_cols(parts[4], proj)
    out_share = lax.psum_scatter(
        partial_value.astype(jnp.bfloat16), "dp", scatter_dimension=1, tiled=True
    ).astype(jnp.float32)
    result = (inputs.astype(jnp.float32) + out_share).astype(jnp.bfloat16)
    carry_mem = jnp.where(decoder, fwd_mem[0], result)
    next_h, next_mem = from_behind((result, carry_mem), "section", 1)
    grad_in = jnp.where(section == first_dec - 1, back_mem[0], back_h[0])
    old_ctx = jnp.where(decoder, saved_mem[0], saved_h[0])
    old_h, old_c, grad_full = (
        lax.all_gather(saved_h[0], "dp", axis=1, tiled=True),
        lax.all_gather(old_ctx, "dp", axis=1, tiled=True),
        lax.all_gather(grad_in, "dp", axis=1, tiled=True),
    )
    hn2_f, inv_h = normalize(old_h.astype(jnp.float32))
    cn2_f, inv_c = normalize(old_c.astype(jnp.float32))
    hn2 = hn2_f.astype(jnp.bfloat16)
    cn2 = cn2_f.astype(jnp.bfloat16)
    q3, kv3, probs, probs_b, mixed = attend(hn2, cn2, proj)
    dmix = jnp.dot(grad_full, proj, preferred_element_type=jnp.float32).astype(jnp.bfloat16)
    dq, dkv = attend_back(q3, kv3, probs, probs_b, dmix)
    grad_w = inner_rows(hn2, dq) + inner_rows(cn2, dkv) + inner_rows(grad_full, mixed)
    back_q = outer_cols(dq, proj)
    back_kv = outer_cols(dkv, proj)
    term_h = back_q + (1.0 - dec_flag) * back_kv
    term_c = dec_flag * back_kv
    full_width = old_h.shape[1]
    share_h, share_c = (
        lax.psum_scatter(term_h.astype(jnp.bfloat16), "dp", scatter_dimension=1, tiled=True).astype(
            jnp.float32
        ),
        lax.psum_scatter(term_c.astype(jnp.bfloat16), "dp", scatter_dimension=1, tiled=True).astype(
            jnp.float32
        ),
    )
    part_h = lax.dynamic_slice_in_dim(hn2_f, start, local_width, 1)
    part_c = lax.dynamic_slice_in_dim(cn2_f, start, local_width, 1)
    stat_h, stat_c = lax.psum(
        (jnp.sum(share_h * part_h, axis=-1), jnp.sum(share_c * part_c, axis=-1)), "dp"
    )
    grad_h = inv_h * (share_h - part_h * (stat_h / full_width)[:, None])
    grad_c = inv_c * (share_c - part_c * (stat_c / full_width)[:, None])
    send_h = (grad_in.astype(jnp.float32) + grad_h).astype(jnp.bfloat16)
    send_mem = jnp.where(decoder, back_mem[0].astype(jnp.float32) + grad_c, 0.0).astype(
        jnp.bfloat16
    )
    prev_h, prev_mem = from_behind((send_h, send_mem), "section", -1)
    squares = grad_w * grad_w
    col_next = BETA * col_stat[0] + (1.0 - BETA) * (jnp.mean(squares, axis=0) + TINY)
    row_part = jnp.sum(squares, axis=1)
    total_cols = proj.shape[1] * lax.axis_size("dp")
    row_total = lax.psum(row_part, "dp")
    row_next = BETA * row_stat[0] + (1.0 - BETA) * (row_total / total_cols + TINY)
    step = grad_w * lax.rsqrt(row_next[:, None] * col_next[None, :] / jnp.mean(row_next))
    total_sq = lax.psum(jnp.sum(step * step), "dp")
    root = jnp.sqrt(total_sq / (full_width * total_cols))
    update = (step / jnp.maximum(1.0, root)).astype(jnp.bfloat16)
    return (
        next_h[None],
        next_mem[None],
        prev_h[None],
        prev_mem[None],
        update[None],
        row_next[None],
        col_next[None],
    )


def solution(mesh):
    in_specs = (
        P("section", None, "dp"),
        P("section", None, "dp"),
        P("section", None, "dp"),
        P("section", None, "dp"),
        P("section", None, "dp"),
        P("section", None, "dp"),
        P("section", None, "dp"),
        P("section", None),
        P("section", "dp"),
        P(),
        P(None, "dp"),
    )
    out_specs = (
        P("section", None, "dp"),
        P("section", None, "dp"),
        P("section", None, "dp"),
        P("section", None, "dp"),
        P("section", None, "dp"),
        P("section", None),
        P("section", "dp"),
    )
    return jax.shard_map(
        on_device, mesh=mesh, in_specs=in_specs, out_specs=out_specs, check_vma=False
    )
```

profile of v0, /device:TPU:1, one launch (start us, length us, event | category | flops | bytes accessed | tf_op | source)
XLA Modules:
  0.0 222.3 jit_solution(13811252869516595260)
XLA Ops:
  14.5 19.1 %all-gather.17.cloned.1.call-done = bf16[1,256,2048]{2,1,0:T(8,128)(2,1)} async-done(((bf16[1,256,1024]{2,1,0:T(8,128)(2,1)}), bf16[1,256,2048]{2,1,0:T(8,128)(2,1)}) %all-gather.17.cloned.1.call-update) | async-done | bytes 1048592 | tf_op jit(solution)/shard_map/all_gather | solution.py:109
  35.1 3.8 %fusion.50 = bf16[256,1024]{1,0:T(8,128)(2,1)S(1)} fusion(bf16[1,2048,1024]{2,1,0:T(8,128)(2,1)} %param.17, bf16[1,256,2048]{2,1,0:T(8,128)(2,1)} %all-gather.17.cloned.1.call-done, f32[256]{0:T(256)S(1)} %add_rsqrt_fusion), kind=kOutput, calls=%fused_computation.65 | convolution fusion | flops 1075576832 | bytes 5768192 | tf_op jit(solution)/shard_map/dot_general | solution.py:42
  39.1 17.3 %all-gather.13.cloned.1.call-done = bf16[1,256,2048]{2,1,0:T(8,128)(2,1)} async-done(((bf16[1,256,1024]{2,1,0:T(8,128)(2,1)}), bf16[1,256,2048]{2,1,0:T(8,128)(2,1)}) %all-gather.13.cloned.1.call-update) | async-done | bytes 1048592 | tf_op jit(solution)/shard_map/all_gather | solution.py:108
  58.0 3.8 %fusion.53 = bf16[256,1024]{1,0:T(8,128)(2,1)S(1)} fusion(bf16[1,2048,1024]{2,1,0:T(8,128)(2,1)} %param.17, bf16[1,256,2048]{2,1,0:T(8,128)(2,1)} %all-gather.13.cloned.1.call-done, f32[256]{0:T(256)S(1)} %add_rsqrt_fusion.1), kind=kOutput, calls=%fused_computation.66 | convolution fusion | flops 1075576832 | bytes 5768192 | tf_op jit(solution)/shard_map/dot_general | solution.py:41
  62.0 17.9 %all-gather.15.cloned.1.call-done = bf16[1,256,2048]{2,1,0:T(8,128)(2,1)} async-done(((bf16[1,256,1024]{2,1,0:T(8,128)(2,1)}), bf16[1,256,2048]{2,1,0:T(8,128)(2,1)}) %all-gather.15.cloned.1.call-update) | async-done | bytes 1048592 | tf_op jit(solution)/shard_map/all_gather | solution.py:110
  79.9 3.8 %fusion.56 = bf16[256,1024]{1,0:T(8,128)(2,1)S(1)} fusion(bf16[1,2048,1024]{2,1,0:T(8,128)(2,1)} %param.17, bf16[1,256,2048]{2,1,0:T(8,128)(2,1)} %all-gather.15.cloned.1.call-done), kind=kOutput, calls=%fused_computation.67 | convolution fusion | flops 1074003968 | bytes 5767168 | tf_op jit(solution)/shard_map/dot_general | solution.py:117
  85.7 2.9 %convolution_convert_fusion.1 = bf16[4,256,256]{2,1,0:T(8,128)(2,1)} fusion(bf16[256,4,256]{0,2,1:T(8,128)(2,1)S(1)} %bitcast.134, f32[4,256,256]{1,2,0:T(8,128)S(1)} %fusion.107, f32[4,256,256]{1,2,0:T(8,128)} %get-tuple-element.19, f32[4,256]{1,0:T(4,128)S(1)} %get-tuple-element.18), kind=kOutput, calls=%fused_computation.59 | convolution fusion | flops 136316160 | bytes 3149824 | tf_op jit(solution)/shard_map/hqk,khd->qhd/dot_general | solution.py:61
  88.6 3.1 %fusion.74 = f32[4,256,256]{2,1,0:T(8,128)} fusion(bf16[256,4,256]{0,2,1:T(8,128)(2,1)S(1)} %bitcast.147, f32[4,256,256]{1,2,0:T(8,128)S(1)} %fusion.107, f32[4,256,256]{1,2,0:T(8,128)} %get-tuple-element.19, f32[4,256]{1,0:T(4,128)S(1)} %get-tuple-element.18), kind=kOutput, calls=%fused_computation.83 | convolution fusion | flops 136054016 | bytes 3674112 | tf_op jit(solution)/shard_map/hqk,qhd->khd/dot_general | solution.py:64
  94.6 3.0 %multiply_convert_fusion = (bf16[256,2048]{1,0:T(8,128)(2,1)}, f32[256,2048]{1,0:T(8,128)}) fusion(f32[]{:T(128)S(6)} %convert_element_type.141, bf16[256,1024]{0,1:T(8,128)(2,1)S(1)} %bitcast.130, bf16[1,2048,1024]{2,1,0:T(8,128)(2,1)S(1)} %copy-done.5), kind=kOutput, calls=%fused_computation.43 | convolution fusion | flops 1074790400 | bytes 7864324 | tf_op jit(solution)/shard_map/dot_general | solution.py:32
  101.9 4.3 %multiply_reduce_fusion.1 = (f32[1024]{0:T(1024)S(1)}, f32[2048]{0:T(1024)S(1)}, f32[2048,1024]{1,0:T(8,128)}) fusion(bf16[256,1024]{0,1:T(8,128)(2,1)S(1)} %bitcast.150, bf16[1,256,2048]{2,1,0:T(8,128)(2,1)S(1)} %copy-done.8, f32[2048,1024]{1,0:T(8,128)S(1)} %fusion.81, f32[2048,1024]{1,0:T(8,128)S(1)} %fusion.84), kind=kOutput, calls=%fused_computation.7 | convolution fusion | flops 1084224512 | bytes 26750976 | tf_op jit(solution)/shard_map/dot_general | solution.py:26
  106.2 3.8 %psum.30 = f32[2048]{0:T(1024)S(1)} all-reduce(f32[2048]{0:T(1024)S(1)} %get-tuple-element.8), channel_id=1, replica_groups=mesh['section'=16,'dp'=2] {'dp'}, use_global_device_ids=true, to_apply=%region_17.18 | all-reduce | flops 2048 | bytes 16384 | tf_op jit(solution)/shard_map/psum | solution.py:149
  112.1 5.7 %fusion.23 = bf16[256,2048]{1,0:T(8,128)(2,1)} fusion(bf16[256,1024]{0,1:T(8,128)(2,1)} %bitcast.141, bf16[1,2048,1024]{2,1,0:T(8,128)(2,1)} %param.17, f32[256,2048]{1,0:T(8,128)} %get-tuple-element.21, f32[]{:T(128)S(6)} %sub.43), kind=kOutput, calls=%fused_computation.35 | convolution fusion | flops 1075314688 | bytes 7864324 | tf_op jit(solution)/shard_map/dot_general | solution.py:32
  118.1 8.4 %all-gather.11.cloned.1.call-done = bf16[256,2048]{1,0:T(8,128)(2,1)} async-done(((bf16[256,1024]{1,0:T(8,128)(2,1)}), bf16[256,2048]{1,0:T(8,128)(2,1)}) %all-gather.11.cloned.1.call-update) | async-done | bytes 1048592 | tf_op jit(solution)/shard_map/all_gather | solution.py:92
  128.1 4.3 %fusion.44 = bf16[256,1024]{1,0:T(8,128)(2,1)} fusion(bf16[1,2048,1024]{2,1,0:T(8,128)(2,1)} %param.17, bf16[256,2048]{1,0:T(8,128)(2,1)S(1)} %copy-done.7, f32[256]{0:T(256)S(1)} %add_rsqrt_fusion.3), kind=kOutput, calls=%fused_computation.63 | convolution fusion | flops 1075576832 | bytes 5768192 | tf_op jit(solution)/shard_map/dot_general | solution.py:42
  134.3 4.1 %fusion.47 = bf16[256,1024]{1,0:T(8,128)(2,1)S(1)} fusion(bf16[1,2048,1024]{2,1,0:T(8,128)(2,1)} %param.17, bf16[256,2048]{1,0:T(8,128)(2,1)} %all-gather.11.cloned.1.call-done, f32[256]{0:T(256)S(1)} %add_rsqrt_fusion.2), kind=kOutput, calls=%fused_computation.64 | convolution fusion | flops 1075576832 | bytes 5768192 | tf_op jit(solution)/shard_map/dot_general | solution.py:41
  142.3 4.5 %fusion.26 = bf16[256,2048]{1,0:T(8,128)(2,1)} fusion(bf16[256,1024]{0,1:T(8,128)(2,1)S(1)} %bitcast.156, bf16[1,2048,1024]{2,1,0:T(8,128)(2,1)} %param.17), kind=kOutput, calls=%fused_computation.36 | convolution fusion | flops 1074266112 | bytes 5767168 | tf_op jit(solution)/shard_map/dot_general | solution.py:32
  146.9 5.8 %multiply_reduce_fusion = f32[]{:T(128)} fusion(f32[2048,1024]{1,0:T(8,128)} %get-tuple-element.22, f32[]{:T(128)S(6)} %div.78, f32[1024]{0:T(1024)S(1)} %bitcast.152, f32[2048]{0:T(1024)S(1)} %get-tuple-element.13), kind=kLoop, calls=%fused_computation.4 | loop fusion | flops 10485759 | bytes 8400904 | tf_op jit(solution)/shard_map/reduce_sum | solution.py:152
  157.5 14.2 %reduce-scatter.6.cloned.1.call-done = bf16[256,1024]{1,0:T(8,128)(2,1)} async-done(((bf16[256,2048]{1,0:T(8,128)(2,1)}), bf16[256,1024]{1,0:T(8,128)(2,1)}) %reduce-scatter.6.cloned.1.call-update) | async-done | bytes 524304 | tf_op jit(solution)/shard_map/reduce_scatter | solution.py:126
  173.3 4.4 %all-reduce = (f32[256]{0:T(256)S(1)}, f32[256]{0:T(256)S(1)}, f32[]{:T(128)}) all-reduce(f32[256]{0:T(256)S(1)} %fusion.59, f32[256]{0:T(256)S(1)} %fusion.63, f32[]{:T(128)} %multiply_reduce_fusion), channel_id=1, replica_groups=mesh['section'=16,'dp'=2] {'dp'}, use_global_device_ids=true, to_apply=%region_12.13 | all-reduce | flops 513 | bytes 4104 | tf_op jit(solution)/shard_map/psum | solution.py:135
  181.1 3.8 %collective-permute-start.3 = (bf16[256,1024]{1,0:T(8,128)(2,1)}, bf16[256,1024]{1,0:T(8,128)(2,1)}, u32[]{:S(2)}, u32[]{:S(2)}) collective-permute-start(bf16[256,1024]{1,0:T(8,128)(2,1)} %fusion.67), channel_id=1, source_target_pairs={{2,0},{4,2},{6,4},{8,6},{10,8},{12,10},{14,12},{16,14},{18,16},{20... | collective-permute-start | bytes 1572872 | tf_op jit(solution)/shard_map/ppermute | solution.py:17
  189.0 5.3 %reduce-scatter.4.cloned.1.call-done = bf16[256,1024]{1,0:T(8,128)(2,1)} async-done(((bf16[256,2048]{1,0:T(8,128)(2,1)}), bf16[256,1024]{1,0:T(8,128)(2,1)}) %reduce-scatter.4.cloned.1.call-update) | async-done | bytes 524304 | tf_op jit(solution)/shard_map/reduce_scatter | solution.py:99
  195.9 3.7 %collective-permute-start = (bf16[256,1024]{1,0:T(8,128)(2,1)S(1)}, bf16[256,1024]{1,0:T(8,128)(2,1)S(1)}, u32[]{:S(2)}, u32[]{:S(2)}) collective-permute-start(bf16[256,1024]{1,0:T(8,128)(2,1)S(1)} %get-tuple-element.15), channel_id=1, source_target_pairs={{0,2},{2,4},{4,6},{6,8},{8,10},{10,12},{12,14},{14,16},{16,18},{18... | collective-permute-start | bytes 1572872 | tf_op jit(solution)/shard_map/ppermute | solution.py:17
  201.5 5.6 %fusion.19 = bf16[1,2048,1024]{2,1,0:T(8,128)(2,1)} fusion(f32[]{:T(128)S(6)} %max.2, f32[2048,1024]{1,0:T(8,128)} %get-tuple-element.22, f32[]{:T(128)S(6)} %div.78, f32[1024]{0:T(1024)S(1)} %bitcast.153, f32[2048]{0:T(1024)S(1)} %get-tuple-element.13), kind=kLoop, calls=%fused_computation.25 | loop fusion | flops 10485760 | bytes 12595208 | tf_op jit(solution)/shard_map/broadcast_in_dim | solution.py:160
  207.1 4.1 %collective-permute-done.1 = bf16[256,1024]{1,0:T(8,128)(2,1)S(1)} collective-permute-done((bf16[256,1024]{1,0:T(8,128)(2,1)S(1)}, bf16[256,1024]{1,0:T(8,128)(2,1)S(1)}, u32[]{:S(2)}, u32[]{:S(2)}) %collective-permute-start.1) | collective-permute-done | bytes 524320 | tf_op jit(solution)/shard_map/ppermute | solution.py:17
  (98 shorter events, 48.9 us)
Async XLA Ops:
  7.2 5.6 %copy-start.10 = (bf16[1,256,1024]{2,1,0:T(8,128)(2,1)S(1)}, bf16[1,256,1024]{2,1,0:T(8,128)(2,1)}, u32[]{:S(2)}) copy-start(bf16[1,256,1024]{2,1,0:T(8,128)(2,1)} %param.11) | copy-start | bytes 1572868
  7.2 5.6 %copy-start.6 = (bf16[1,256,1024]{2,1,0:T(8,128)(2,1)S(1)}, bf16[1,256,1024]{2,1,0:T(8,128)(2,1)}, u32[]{:S(2)}) copy-start(bf16[1,256,1024]{2,1,0:T(8,128)(2,1)} %param.12) | copy-start | bytes 1572868
  7.2 5.6 %copy-start.9 = (bf16[256,1024]{1,0:T(8,128)(2,1)S(1)}, bf16[256,1024]{1,0:T(8,128)(2,1)}, u32[]{:S(2)}) copy-start(bf16[256,1024]{1,0:T(8,128)(2,1)} %param.21) | copy-start | bytes 1572868
  7.2 26.4 %all-gather.17.cloned.1.call-start = ((), (), s32[]{:S(2)}) async-start(), calls=%async_computation.10 | async-start | bytes 1572864 | tf_op jit(solution)/shard_map/all_gather | solution.py:109
  8.0 6.5 %copy-start.14 = (f32[1,2048]{1,0:T(1,128)S(1)}, f32[1,2048]{1,0:T(1,128)}, u32[]{:S(2)}) copy-start(f32[1,2048]{1,0:T(1,128)} %param.18) | copy-start | bytes 24580
  9.9 46.5 %all-gather.13.cloned.1.call-start = ((), (), s32[]{:S(2)}) async-start(), calls=%async_computation.8 | async-start | bytes 1572864 | tf_op jit(solution)/shard_map/all_gather | solution.py:108
  10.7 69.2 %all-gather.15.cloned.1.call-start = ((), (), s32[]{:S(2)}) async-start(), calls=%async_computation.9 | async-start | bytes 1572864 | tf_op jit(solution)/shard_map/all_gather | solution.py:110
  12.7 97.3 %all-gather.9.cloned.1.call-start = ((), (), s32[]{:S(2)}) async-start(), calls=%async_computation.3 | async-start | bytes 1572864 | tf_op jit(solution)/shard_map/all_gather | solution.py:93
  13.8 112.7 %all-gather.11.cloned.1.call-start = ((), (), s32[]{:S(2)}) async-start(), calls=%async_computation.4 | async-start | bytes 1572864 | tf_op jit(solution)/shard_map/all_gather | solution.py:92
  14.4 141.4 %reduce-scatter.8.cloned.1.call-start = ((), (), s32[]{:S(2)}) async-start(), calls=%async_computation.7 | async-start | bytes 1572864 | tf_op jit(solution)/shard_map/reduce_scatter | solution.py:129
  94.6 3.2 %copy-start = (bf16[1,256,2048]{2,1,0:T(8,128)(2,1)S(1)}, bf16[1,256,2048]{2,1,0:T(8,128)(2,1)}, u32[]{:S(2)}) copy-start(bf16[1,256,2048]{2,1,0:T(8,128)(2,1)} %all-gather.17.cloned.1.call-done) | copy-start | bytes 3145732
  97.6 74.2 %reduce-scatter.6.cloned.1.call-start = ((), (), s32[]{:S(2)}) async-start(), calls=%async_computation.6 | async-start | bytes 1572864 | tf_op jit(solution)/shard_map/reduce_scatter | solution.py:126
  112.1 89.4 %copy-start.12 = (f32[2048]{0:T(1024)}, f32[2048]{0:T(1024)S(1)}, u32[]{:S(2)}) copy-start(f32[2048]{0:T(1024)S(1)} %get-tuple-element.13) | copy-start | bytes 24580
  112.1 15.9 %copy-start.7 = (bf16[256,2048]{1,0:T(8,128)(2,1)S(1)}, bf16[256,2048]{1,0:T(8,128)(2,1)}, u32[]{:S(2)}) copy-start(bf16[256,2048]{1,0:T(8,128)(2,1)} %all-gather.9.cloned.1.call-done) | copy-start | bytes 3145732
  117.8 76.5 %reduce-scatter.4.cloned.1.call-start = ((), (), s32[]{:S(2)}) async-start(), calls=%async_computation.5 | async-start | bytes 1572864 | tf_op jit(solution)/shard_map/reduce_scatter | solution.py:99
  134.3 4.7 %copy-start.15 = (f32[1,1024]{1,0:T(1,128)S(1)}, f32[1,1024]{1,0:T(1,128)}, u32[]{:S(2)}) copy-start(f32[1,1024]{1,0:T(1,128)} %param.19) | copy-start | bytes 12292
  139.0 62.5 %copy-start.13 = (f32[1,1024]{1,0:T(1,128)}, f32[1,1024]{1,0:T(1,128)S(1)}, u32[]{:S(2)}) copy-start(f32[1,1024]{1,0:T(1,128)S(1)} %multiply_add_fusion.1) | copy-start | bytes 12292
  154.3 30.6 %copy-start.3 = (bf16[1,256,1024]{2,1,0:T(8,128)(2,1)S(1)}, bf16[1,256,1024]{2,1,0:T(8,128)(2,1)}, u32[]{:S(2)}) copy-start(bf16[1,256,1024]{2,1,0:T(8,128)(2,1)} %broadcast_select_fusion.1) | copy-start | bytes 1572868
  155.8 29.1 %copy-start.2 = (f32[256,2048]{1,0:T(8,128)S(1)}, f32[256,2048]{1,0:T(8,128)}, u32[]{:S(2)}) copy-start(f32[256,2048]{1,0:T(8,128)} %convert_multiply_fusion) | copy-start | bytes 6291460
  155.8 38.5 %copy-start.4 = (bf16[256,1024]{1,0:T(8,128)(2,1)S(1)}, bf16[256,1024]{1,0:T(8,128)(2,1)}, u32[]{:S(2)}) copy-start(bf16[256,1024]{1,0:T(8,128)(2,1)} %get-tuple-element.17) | copy-start | bytes 1572868
  181.1 26.0 %collective-permute-start.3 = (bf16[256,1024]{1,0:T(8,128)(2,1)}, bf16[256,1024]{1,0:T(8,128)(2,1)}, u32[]{:S(2)}, u32[]{:S(2)}) collective-permute-start(bf16[256,1024]{1,0:T(8,128)(2,1)} %fusion.67), channel_id=1, source_target_pairs={{2,0},{4,2},{6,4},{8,6},{10,8},{12,10},{14,12},{16,14},{18,16},{20... | collective-permute-start | bytes 1572872 | tf_op jit(solution)/shard_map/ppermute | solution.py:17
  187.1 20.0 %collective-permute-start.2 = (bf16[256,1024]{1,0:T(8,128)(2,1)}, bf16[256,1024]{1,0:T(8,128)(2,1)S(1)}, u32[]{:S(2)}, u32[]{:S(2)}) collective-permute-start(bf16[256,1024]{1,0:T(8,128)(2,1)} %fusion.62), channel_id=1, source_target_pairs={{2,0},{4,2},{6,4},{8,6},{10,8},{12,10},{14,12},{16,14},{18,16},{20... | collective-permute-start | bytes 1572872 | tf_op jit(solution)/shard_map/ppermute | solution.py:17
  195.9 11.3 %collective-permute-start = (bf16[256,1024]{1,0:T(8,128)(2,1)S(1)}, bf16[256,1024]{1,0:T(8,128)(2,1)S(1)}, u32[]{:S(2)}, u32[]{:S(2)}) collective-permute-start(bf16[256,1024]{1,0:T(8,128)(2,1)S(1)} %get-tuple-element.15), channel_id=1, source_target_pairs={{0,2},{2,4},{4,6},{6,8},{8,10},{10,12},{12,14},{14,16},{16,18},{18... | collective-permute-start | bytes 1572872 | tf_op jit(solution)/shard_map/ppermute | solution.py:17
  199.5 11.7 %collective-permute-start.1 = (bf16[256,1024]{1,0:T(8,128)(2,1)S(1)}, bf16[256,1024]{1,0:T(8,128)(2,1)S(1)}, u32[]{:S(2)}, u32[]{:S(2)}) collective-permute-start(bf16[256,1024]{1,0:T(8,128)(2,1)S(1)} %get-tuple-element.14), channel_id=1, source_target_pairs={{0,2},{2,4},{4,6},{6,8},{8,10},{10,12},{12,14},{14,16},{16,18},{18... | collective-permute-start | bytes 1572872 | tf_op jit(solution)/shard_map/ppermute | solution.py:17
  (5 other events, 8.6 us)
Sparse Core Ops, SparseCore 0:
  10.2 23.3 all-gather.16
  35.1 21.2 all-gather.12
  58.6 21.2 all-gather.14
  81.9 21.2 all-gather.8
  105.2 21.2 all-gather.10
  128.6 20.3 reduce-scatter.7
  151.3 20.3 reduce-scatter.5
  174.0 20.3 reduce-scatter.3
where the time goes:
time: 224 us; the launch traced here: 222 us
  waiting for transfers between devices  87.7 us (39%)
  matrix products  54.1 us (24%)
  other arithmetic  35.7 us (16%)
  between operations  16.6 us (7%)
  starting transfers between devices  12 us (5%)
  blocking collectives  8.24 us (4%)
  local copies, waits for them, and re-layouts  7.85 us (4%)
    all_gather x1, waiting for transfers between devices, on_device(): lax.all_gather(old_ctx, 'dp', axis=1, tiled=True)  19.1 us
    all_gather x1, waiting for transfers between devices, on_device(): lax.all_gather(grad_in, 'dp', axis=1, tiled=True)  17.9 us
    all_gather x1, waiting for transfers between devices, on_device(): lax.all_gather(saved_h[0], 'dp', axis=1, tiled=True)  17.3 us
    reduce_scatter x1, waiting for transfers between devices, on_device(): lax.psum_scatter(term_h.astype(jnp.bfloat16), 'dp', scatter_dimension=1,...  14.2 us
    dot_general x3, matrix products, outer_cols(): lax.dot_general(left, right, (((1,), (1,)), ((), ())), preferred_element_...  13.2 us
    ppermute x4, starting transfers between devices, from_behind(): return lax.ppermute(x, axis, pairs)  11.3 us
    all_gather x1, waiting for transfers between devices, on_device(): lax.all_gather(inputs, 'dp', axis=1, tiled=True)  8.43 us
    dot_general x2, matrix products, attend(): jnp.dot(cn, weight, preferred_element_type=jnp.float32).astype(jnp.bfloat16)  8.11 us
  transfers between devices with their start and end apart: 12, of which 7 were waited for; matrix products, arithmetic and copies ran while one was open for 40% of the time, Pallas kernels for 0%

commit v1 on v0

v1 whole, which is shorter than its diff:
```python
import functools

import jax
import jax.numpy as jnp
from jax import lax
from jax.experimental import pallas as pl
from jax.experimental.pallas import tpu as pltpu
from jax.sharding import PartitionSpec as P

HD = 256
EPS = 1e-06
BETA = 0.8
TINY = 1e-30
SCALE = 1.0 / HD**0.5
MESH = pl.DeviceIdType.MESH
F32 = jnp.float32
BF16 = jnp.bfloat16
MIB = 1024 * 1024


def dot_nn(a, b):
    return lax.dot_general(a, b, (((1,), (0,)), ((), ())), preferred_element_type=F32)


def dot_nt(a, b):
    return lax.dot_general(a, b, (((1,), (1,)), ((), ())), preferred_element_type=F32)


def dot_tn(a, b):
    return lax.dot_general(a, b, (((0,), (0,)), ((), ())), preferred_element_type=F32)


def lanes_to_rows(first, second):
    rows = first.shape[0]
    lane = lax.broadcasted_iota(jnp.int32, (rows, 128), 1)
    both = jnp.where(lane == 0, first, second)
    return jnp.transpose(both)[0:8]


def rows_to_lanes(row):
    return jnp.transpose(jnp.broadcast_to(row, (128, row.shape[1])))


def kernel(
    n, sections, rows, width, cols, tile,
    fwd_h, fwd_mem, saved_h, saved_mem, back_h, back_mem, weight, row_stat, col_stat, count, target,
    next_h, got_mem, prev_h, prev_mem, update, row_new, col_new,
    proj, sh, sm, xh, xm, tmp, left, fleft, qkv, probs, right, fmix,
    th, tc, out, th_in, tc_in, out_in, inv, stats, grad, sums, acc, upd, send_h, send_m, send_y,
    local_sem, gather_s, gather_r, part_s, part_r, small_s, small_r, sec_s, sec_r,
):
    me = lax.axis_index("dp")
    s = lax.axis_index("section")
    tiles = width // tile
    heads = cols // HD
    full = n * width
    r2, r3 = 2 * rows, 3 * rows
    first_dec = count[0]
    dec = (s >= first_dec).astype(jnp.int32)
    is_first = (s == first_dec).astype(jnp.int32)
    is_last_enc = (s == first_dec - 1).astype(jnp.int32)
    own_tmp = [tmp.at[i] for i in range(4)]

    def peer(k):
        return lax.rem(me + k, n)

    def source(k):
        return lax.rem(me + n - k, n)

    loads = [
        (back_h.at[0], own_tmp[0]),
        (back_mem.at[0], own_tmp[1]),
        (fwd_h.at[0], own_tmp[2]),
        (target, own_tmp[3]),
        (saved_h.at[0], sh.at[me]),
        (saved_mem.at[0], sm.at[me]),
        (weight.at[0], proj),
        (fwd_mem.at[0], xm.at[me]),
    ]
    loads = [pltpu.make_async_copy(a, b, local_sem.at[i]) for i, (a, b) in enumerate(loads)]
    for load in loads:
        load.start()

    barrier = pltpu.get_barrier_semaphore()
    for k in range(1, n):
        pl.semaphore_signal(barrier, 1, device_id={"dp": peer(k)}, device_id_type=MESH)

    @pl.when(s > 0)
    def _():
        pl.semaphore_signal(barrier, 1, device_id={"section": s - 1}, device_id_type=MESH)

    @pl.when(s < sections - 1)
    def _():
        pl.semaphore_signal(barrier, 1, device_id={"section": s + 1}, device_id_type=MESH)

    ends = (s > 0).astype(jnp.int32) + (s < sections - 1).astype(jnp.int32)
    pl.semaphore_wait(barrier, n - 1 + ends)

    def to_peer(src, dst, send, recv, k):
        return pltpu.make_async_remote_copy(
            src, dst, send, recv, device_id={"dp": peer(k)}, device_id_type=MESH
        )

    def gather_start(i, src, slot):
        for k in range(1, n):
            to_peer(src, slot(me), gather_s.at[i, k - 1], gather_r.at[i, k - 1], k).start()

    def gather_wait(i, src, slot):
        for k in range(1, n):
            to_peer(src, slot(me), gather_s.at[i, k - 1], gather_r.at[i, k - 1], k).wait_send()
            got = slot(source(k))
            to_peer(got, got, gather_s.at[i, k - 1], gather_r.at[i, k - 1], k).wait_recv()

    def g_slot(p):
        return left.at[p, pl.ds(r2, rows)]

    gather_start(0, saved_h.at[0], lambda p: sh.at[p])
    gather_start(1, saved_mem.at[0], lambda p: sm.at[p])

    def section_copy(i, t, src, dst, by):
        return pltpu.make_async_remote_copy(
            src, dst, sec_s.at[i, t], sec_r.at[i, t],
            device_id={"section": s + by}, device_id_type=MESH,
        )

    @pl.when(s < sections - 1)
    def _():
        section_copy(0, 0, fwd_mem.at[0], got_mem.at[0], 1).start()

    def select(flag, yes, no, dst):
        step = 32

        def body(i, carry):
            at = pl.ds(pl.multiple_of(i * step, step), step)
            mask = jnp.full((step, width), flag, jnp.int32) > 0
            dst[at, :] = jnp.where(mask, yes[at, :].astype(F32), no[at, :].astype(F32)).astype(BF16)
            return carry

        lax.fori_loop(0, rows // step, body, 0)

    for i in range(4):
        loads[i].wait()
    select(is_last_enc, own_tmp[1], own_tmp[0], left.at[me, pl.ds(r2, rows)])
    select(is_first, own_tmp[3], own_tmp[2], xh.at[me])

    def normalize(h_ref, m_ref, dst, keep):
        step = 32

        def body(i, carry):
            at = pl.ds(pl.multiple_of(i * step, step), step)
            at_c = pl.ds(pl.multiple_of(rows + i * step, step), step)
            h = [h_ref[p, at, :].astype(F32) for p in range(n)]
            mask = jnp.full((step, width), dec, jnp.int32) > 0
            c = [jnp.where(mask, m_ref[p, at, :].astype(F32), h[p]) for p in range(n)]
            for j, (v, where) in enumerate(((h, at), (c, at_c))):
                total = sum(jnp.sum(x * x, axis=1, keepdims=True) for x in v)
                r = lax.rsqrt(total / full + EPS)
                for p in range(n):
                    dst[p, where, :] = (v[p] * r).astype(BF16)
                if keep:
                    inv[j, at, :] = jnp.broadcast_to(r, (step, 128))
            return carry

        lax.fori_loop(0, rows // step, body, 0)

    def head_cols(h):
        return pl.ds(pl.multiple_of(h * HD, HD), HD)

    def project(src, lo, size, at):
        return sum(
            dot_nn(src[p, lo : lo + size, :], proj[p * width : (p + 1) * width, at])
            for p in range(n)
        )

    def softmax(q, kv):
        score = dot_nt(q, kv) * SCALE
        e = jnp.exp(score - jnp.max(score, axis=1, keepdims=True))
        return e / jnp.sum(e, axis=1, keepdims=True)

    loads[4].wait()
    loads[5].wait()
    gather_wait(0, saved_h.at[0], lambda p: sh.at[p])
    gather_start(2, g_slot(me), g_slot)
    gather_wait(1, saved_mem.at[0], lambda p: sm.at[p])
    gather_start(3, xh.at[me], lambda p: xh.at[p])
    normalize(sh, sm, left, True)
    loads[6].wait()

    def attend_body(h, carry):
        at = head_cols(h)
        both = project(left, 0, r2, at).astype(BF16)
        qkv[:, at] = both
        q, kv = both[:rows], both[rows:]
        p = softmax(q, kv)
        probs[h] = p
        right[r2:r3, at] = dot_nn(p.astype(BF16), kv).astype(BF16)
        return carry

    lax.fori_loop(0, heads, attend_body, 0)

    gather_wait(2, g_slot(me), g_slot)
    gather_start(4, fwd_mem.at[0], lambda p: xm.at[p])

    def back_body(h, carry):
        stat_q, stat_k = carry
        at = head_cols(h)
        dmix = project(left, r2, rows, at).astype(BF16)
        q, kv = qkv[0:rows, at], qkv[rows:r2, at]
        p = probs[h]
        dprobs = dot_nt(dmix, kv)
        dval = dot_tn(p.astype(BF16), dmix)
        inner = jnp.sum(dprobs * p, axis=1, keepdims=True)
        dscore = (p * (dprobs - inner) * SCALE).astype(BF16)
        dq = dot_nn(dscore, kv).astype(BF16)
        dkv = (dot_tn(dscore, q) + dval).astype(BF16)
        right[0:rows, at] = dq
        right[rows:r2, at] = dkv
        stat_q += jnp.sum(dq.astype(F32) * q.astype(F32), axis=1, keepdims=True)
        stat_k += jnp.sum(dkv.astype(F32) * kv.astype(F32), axis=1, keepdims=True)
        return stat_q, stat_k

    zero_col = jnp.zeros((rows, 1), F32)
    stat_q, stat_k = lax.fori_loop(0, heads, back_body, (zero_col, zero_col))
    decf = jnp.full((rows, 1), dec, jnp.int32).astype(F32)
    stats[me] = lanes_to_rows(stat_q + (1.0 - decf) * stat_k, decf * stat_k)
    for k in range(1, n):
        to_peer(stats.at[me], stats.at[me], small_s.at[0, k - 1], small_r.at[0, k - 1], k).start()

    def row_tile(p, t):
        return pl.ds(pl.multiple_of(p * width + t * tile, tile), tile)

    def terms(p, t, to_h, to_c):
        both = dot_nt(right[0:r2, :], proj[row_tile(p, t), :])
        bq, bk = both[:rows], both[rows:]
        flag = jnp.full((rows, tile), dec, jnp.int32).astype(F32)
        to_h[...] = (bq + (1.0 - flag) * bk).astype(BF16)
        to_c[...] = (flag * bk).astype(BF16)

    def part_copy(i, k, t, src, dst):
        return to_peer(
            src.at[k - 1, t], dst.at[k, t], part_s.at[i, k - 1, t], part_r.at[i, k - 1, t], k
        )

    for k in range(1, n):
        for t in range(tiles):
            terms(peer(k), t, th.at[k - 1, t], tc.at[k - 1, t])
            part_copy(0, k, t, th, th_in).start()
            part_copy(1, k, t, tc, tc_in).start()

    def own_terms(t, carry):
        terms(me, t, th_in.at[0, t], tc_in.at[0, t])
        return carry

    lax.fori_loop(0, tiles, own_terms, 0)

    loads[7].wait()
    gather_wait(3, xh.at[me], lambda p: xh.at[p])
    gather_wait(4, fwd_mem.at[0], lambda p: xm.at[p])
    normalize(xh, xm, fleft, False)

    def forward_body(h, carry):
        at = head_cols(h)
        both = project(fleft, 0, r2, at).astype(BF16)
        kv = both[rows:]
        p = softmax(both[:rows], kv).astype(BF16)
        fmix[:, at] = dot_nn(p, kv).astype(BF16)
        return carry

    lax.fori_loop(0, heads, forward_body, 0)
    for k in range(1, n):
        for t in range(tiles):
            out[k - 1, t] = dot_nt(fmix[...], proj[row_tile(peer(k), t), :]).astype(BF16)
            part_copy(2, k, t, out, out_in).start()

    def own_out(t, carry):
        out_in[0, t] = dot_nt(fmix[...], proj[row_tile(me, t), :]).astype(BF16)
        return carry

    lax.fori_loop(0, tiles, own_out, 0)

    acc[...] = jnp.zeros_like(acc)

    def grad_body(f, carry):
        p, t = f // tiles, f % tiles
        tl = left[p, :, pl.ds(pl.multiple_of(t * tile, tile), tile)]
        g = dot_tn(tl, right[...])
        grad[pl.ds(pl.multiple_of(f * tile, tile), tile), :] = g
        acc[...] += jnp.sum((g * g).reshape(tile // 8, 8, cols), axis=0)
        return carry

    lax.fori_loop(0, n * tiles, grad_body, 0)
    col = BETA * col_stat[...] + (1.0 - BETA) * (
        jnp.sum(acc[...], axis=0, keepdims=True) / full + TINY
    )
    col_new[...] = col
    inv_col = 1.0 / col

    step = 128

    def sums_body(i, carry):
        at = pl.ds(pl.multiple_of(i * step, step), step)
        g = grad[at, :]
        g = g * g
        sums[me, :, at] = lanes_to_rows(
            jnp.sum(g, axis=1, keepdims=True), jnp.sum(g * inv_col, axis=1, keepdims=True)
        )
        return carry

    lax.fori_loop(0, full // step, sums_body, 0)
    for k in range(1, n):
        to_peer(sums.at[me], sums.at[me], small_s.at[1, k - 1], small_r.at[1, k - 1], k).start()

    def small_wait(i, ref):
        for k in range(1, n):
            to_peer(
                ref.at[me], ref.at[me], small_s.at[i, k - 1], small_r.at[i, k - 1], k
            ).wait_send()
            got = ref.at[source(k)]
            to_peer(got, got, small_s.at[i, k - 1], small_r.at[i, k - 1], k).wait_recv()

    small_wait(0, stats)
    stat = sum(stats[p] for p in range(n)) / full
    stat_h, stat_c = rows_to_lanes(stat[0:1])[:, 0:1], rows_to_lanes(stat[1:2])[:, 0:1]

    def tile_cols(t):
        return slice(t * tile, (t + 1) * tile)

    for t in range(tiles):
        for k in range(1, n):
            part_copy(0, k, t, th, th_in).wait()
            part_copy(1, k, t, tc, tc_in).wait()
        share_h = sum(th_in[k, t].astype(F32) for k in range(n))
        share_c = sum(tc_in[k, t].astype(F32) for k in range(n))
        at = tile_cols(t)
        inv_h, inv_c = inv[0][:, 0:1], inv[1][:, 0:1]
        grad_h = inv_h * (share_h - sh[me, :, at].astype(F32) * inv_h * stat_h)
        grad_c = inv_c * (share_c - sm[me, :, at].astype(F32) * inv_c * stat_c)
        send_h[t] = (left[me, r2:r3, at].astype(F32) + grad_h).astype(BF16)
        mask = jnp.full((rows, tile), dec, jnp.int32) > 0
        send_m[t] = jnp.where(mask, own_tmp[1][:, at].astype(F32) + grad_c, 0.0).astype(BF16)

        @pl.when(s > 0)
        def _():
            section_copy(1, t, send_h.at[t], prev_h.at[0, :, pl.ds(t * tile, tile)], -1).start()
            section_copy(2, t, send_m.at[t], prev_mem.at[0, :, pl.ds(t * tile, tile)], -1).start()

    for t in range(tiles):
        for k in range(1, n):
            part_copy(2, k, t, out, out_in).wait()
        at = tile_cols(t)
        share = sum(out_in[k, t].astype(F32) for k in range(n))
        send_y[t] = (xh[me, :, at].astype(F32) + share).astype(BF16)

        @pl.when(s < sections - 1)
        def _():
            section_copy(3, t, send_y.at[t], next_h.at[0, :, pl.ds(t * tile, tile)], 1).start()

    small_wait(1, sums)
    total = sum(sums[p] for p in range(n))
    row = BETA * row_stat[...] + (1.0 - BETA) * (total[0:1] / (n * cols) + TINY)
    row_new[...] = row
    mean_row = jnp.sum(row, axis=1, keepdims=True) / full
    total_sq = mean_row * jnp.sum(total[1:2] / row, axis=1, keepdims=True)
    root = jnp.sqrt(total_sq / (full * (n * cols)))
    sums[me, 0:1, :] = lax.rsqrt(row) * (jnp.sqrt(mean_row) / jnp.maximum(1.0, root))
    root_col = lax.rsqrt(col)

    def update_copy(at, i):
        return pltpu.make_async_copy(upd.at[at], update.at[0, at], local_sem.at[i])

    def update_body(i, carry):
        at = pl.ds(pl.multiple_of(i * step, step), step)
        factor = rows_to_lanes(sums[me, 0:1, at])[:, 0:1]
        upd[at, :] = (grad[at, :] * factor * root_col).astype(BF16)
        return carry

    pieces = 4
    size = full // pieces
    for j in range(pieces):
        lax.fori_loop(j * (size // step), (j + 1) * (size // step), update_body, 0)
        update_copy(pl.ds(j * size, size), 8 + j).start()

    @pl.when(s == 0)
    def _():
        own_tmp[0][...] = jnp.zeros((rows, width), BF16)
        for i, dst in enumerate((next_h, got_mem)):
            pltpu.make_async_copy(own_tmp[0], dst.at[0], local_sem.at[i]).start()
        for i, dst in enumerate((next_h, got_mem)):
            pltpu.make_async_copy(own_tmp[0], dst.at[0], local_sem.at[i]).wait()

    @pl.when(s == sections - 1)
    def _():
        own_tmp[0][...] = jnp.zeros((rows, width), BF16)
        for i, dst in enumerate((prev_h, prev_mem)):
            pltpu.make_async_copy(own_tmp[0], dst.at[0], local_sem.at[i]).start()
        for i, dst in enumerate((prev_h, prev_mem)):
            pltpu.make_async_copy(own_tmp[0], dst.at[0], local_sem.at[i]).wait()

    @pl.when(s < sections - 1)
    def _():
        section_copy(0, 0, fwd_mem.at[0], got_mem.at[0], 1).wait_send()
        for t in range(tiles):
            at = pl.ds(t * tile, tile)
            section_copy(3, t, send_y.at[t], next_h.at[0, :, at], 1).wait_send()
            section_copy(1, t, send_h.at[t], prev_h.at[0, :, at], 1).wait_recv()
            section_copy(2, t, send_m.at[t], prev_mem.at[0, :, at], 1).wait_recv()

    @pl.when(s > 0)
    def _():
        section_copy(0, 0, fwd_mem.at[0], got_mem.at[0], -1).wait_recv()
        for t in range(tiles):
            at = pl.ds(t * tile, tile)
            section_copy(3, t, send_y.at[t], next_h.at[0, :, at], -1).wait_recv()
            section_copy(1, t, send_h.at[t], prev_h.at[0, :, at], -1).wait_send()
            section_copy(2, t, send_m.at[t], prev_mem.at[0, :, at], -1).wait_send()

    for j in range(pieces):
        update_copy(pl.ds(j * size, size), 8 + j).wait()


def on_device(
    n, sections,
    fwd_h, fwd_mem, saved_h, saved_mem, back_h, back_mem, weight, row_stat, col_stat, enc_count,
    target_embed,
):
    rows, width = fwd_h.shape[1:]
    cols = weight.shape[2]
    full = n * width
    tile = min(256, width)
    tiles = width // tile
    heads = cols // HD
    hbm = pl.BlockSpec(memory_space=pl.ANY)
    vmem = pl.BlockSpec(memory_space=pltpu.VMEM)
    smem = pl.BlockSpec(memory_space=pltpu.SMEM)
    act = jax.ShapeDtypeStruct((1, rows, width), BF16)
    dma = pltpu.SemaphoreType.DMA
    parts = pltpu.VMEM((n, tiles, rows, tile), BF16)
    others = pltpu.VMEM((n - 1, tiles, rows, tile), BF16)
    stored = pltpu.VMEM((n, rows, width), BF16)
    result = pltpu.VMEM((tiles, rows, tile), BF16)
    next_h, got_mem, prev_h, prev_mem, update, row_new, col_new = pl.pallas_call(
        functools.partial(kernel, n, sections, rows, width, cols, tile),
        out_shape=(
            act, act, act, act,
            jax.ShapeDtypeStruct((1, full, cols), BF16),
            jax.ShapeDtypeStruct((1, full), F32),
            jax.ShapeDtypeStruct((1, cols), F32),
        ),
        in_specs=[hbm] * 7 + [vmem, vmem, smem, hbm],
        out_specs=[hbm] * 5 + [vmem, vmem],
        scratch_shapes=[
            pltpu.VMEM((full, cols), BF16),
            stored, stored, stored, stored,
            pltpu.VMEM((4, rows, width), BF16),
            pltpu.VMEM((n, 3 * rows, width), BF16),
            pltpu.VMEM((n, 2 * rows, width), BF16),
            pltpu.VMEM((2 * rows, cols), BF16),
            pltpu.VMEM((heads, rows, rows), F32),
            pltpu.VMEM((3 * rows, cols), BF16),
            pltpu.VMEM((rows, cols), BF16),
            others, others, others, parts, parts, parts,
            pltpu.VMEM((2, rows, 128), F32),
            pltpu.VMEM((n, 8, rows), F32),
            pltpu.VMEM((full, cols), F32),
            pltpu.VMEM((n, 8, full), F32),
            pltpu.VMEM((8, cols), F32),
            pltpu.VMEM((full, cols), BF16),
            result, result, result,
            dma((12,)),
            dma((5, n - 1)), dma((5, n - 1)),
            dma((3, n - 1, tiles)), dma((3, n - 1, tiles)),
            dma((2, n - 1)), dma((2, n - 1)),
            dma((4, tiles)), dma((4, tiles)),
        ],
        compiler_params=pltpu.CompilerParams(
            collective_id=0, has_side_effects=True, vmem_limit_bytes=58 * MIB
        ),
    )(
        fwd_h, fwd_mem, saved_h, saved_mem, back_h, back_mem, weight, row_stat, col_stat,
        enc_count, target_embed,
    )
    before_dec = lax.axis_index("section") - 1 >= enc_count[0]
    next_mem = jnp.where(before_dec, got_mem, next_h)
    return (next_h, next_mem, prev_h, prev_mem, update, row_new, col_new)


def solution(mesh):
    act = P("section", None, "dp")
    in_specs = (
        act, act, act, act, act, act, act, P("section", None), P("section", "dp"), P(), P(None, "dp"),
    )
    out_specs = (act, act, act, act, act, P("section", None), P("section", "dp"))
    body = functools.partial(on_device, mesh.shape["dp"], mesh.shape["section"])
    return jax.shard_map(
        body, mesh=mesh, in_specs=in_specs, out_specs=out_specs, check_vma=False
    )
```

time: 224 us -> 114 us (0.51)
  Pallas kernels: 0 us -> 102 us
  waiting for transfers between devices: 87.7 us -> 0 us
  matrix products: 54.1 us -> 0 us
  other arithmetic: 35.7 us -> 2.05 us
  between operations: 16.6 us -> 1.31 us
  starting transfers between devices: 12 us -> 0 us
  blocking collectives: 8.24 us -> 0 us
    pallas_call x0 -> x1, Pallas kernels: none -> 102 us  [on_device(): pl.pallas_call(functools.partial(kernel, n, sections, rows, width, cols,...]
    all_gather x5 -> x0, waiting for transfers between devices: 62.7 us -> none  [the longest x1 19.1 us: on_device(): lax.all_gather(old_ctx, 'dp', axis=1, tiled=True)]
    dot_general x18 -> x0, matrix products: 52.1 us -> none  [the longest x3 13.2 us: outer_cols(): lax.dot_general(left, right, (((1,), (1,)), ((), ())), preferred_element_...]
    reduce_scatter x3 -> x0, waiting for transfers between devices: 19.5 us -> none  [the longest x1 14.2 us: on_device(): lax.psum_scatter(term_h.astype(jnp.bfloat16), 'dp', scatter_dimension=1,...]
    reduce_sum x8 -> x0, other arithmetic: 15.7 us -> none  [the longest x4 6.04 us: normalize(): inv = lax.rsqrt(jnp.mean(values * values, axis=-1, keepdims=True) + EPS)]
    ppermute x4 -> x0, starting transfers between devices: 11.3 us -> none  [from_behind(): return lax.ppermute(x, axis, pairs)]
    psum x2 -> x0, blocking collectives: 8.24 us -> none  [the longest x1 4.43 us: on_device(): lax.psum((jnp.sum(share_h * part_h, axis=-1), jnp.sum(share_c * part_c, a...]
    broadcast_in_dim x1 -> x0, other arithmetic: 5.63 us -> none  [on_device(): update[None]]
  transfers between devices with their start and end apart: 12 -> 0, of which waited for: 7 -> 0; matrix products, arithmetic and copies ran while one was open for 40% -> 0% of each run, Pallas kernels for 0% -> 0%
where the time goes in v1:
time: 114 us
  Pallas kernels  102 us (89%)
  local copies, waits for them, and re-layouts  8.82 us (8%)
  other arithmetic  2.05 us (2%)
  between operations  1.31 us (1%)
    pallas_call x1, Pallas kernels, on_device(): pl.pallas_call(functools.partial(kernel, n, sections, rows, width, cols,...  102 us
    unnamed x12, local copies, waits for them, and re-layouts  8.82 us

profile of v1, /device:TPU:1, one launch (start us, length us, event | category | flops | bytes accessed | tf_op | source)
XLA Modules:
  0.0 113.9 jit_solution(3797799129009149534)
XLA Ops:
  1.3 101.8 %shard_map.162 = (bf16[1,256,1024]{2,1,0:T(8,128)(2,1)}, bf16[1,256,1024]{2,1,0:T(8,128)(2,1)}, bf16[1,256,1024]{2,1,0:T(8,128)(2,1)}, bf16[1,256,1024]{2,1,0:T(...) custom-call(bf16[1,256,1024]{2,1,0:T(8,128)(2,1)} %fwd_h.1, ...), custom_call_target="tpu_custom_call" | custom-call | tf_op jit(solution)/shard_map/pallas_call | solution.py:441
  103.1 0.0 copy-start
  103.1 2.1 %broadcast_select_fusion = bf16[1,256,1024]{2,1,0:T(8,128)(2,1)} fusion(bf16[1,256,1024]{2,1,0:T(8,128)(2,1)} %get-tuple-element.15, bf16[1,256,1024]{2,1,0:T(8,128)(2,1)} %get-tuple-element.28, pred[]{:T(512)S(6)} %ge.3), kind=kLoop, calls=%fused_computation | loop fusion | flops 262144 | bytes 1572865 | tf_op jit(solution)/shard_map/jit(_where)/select_n | solution.py:483
  105.1 1.9 %copy.25 = bf16[1,256,1024]{2,1,0:T(8,128)(2,1)} copy(bf16[1,256,1024]{2,1,0:T(8,128)(2,1)} %get-tuple-element.28) | data formatting | bytes 1048576
  107.0 1.9 %copy.26 = bf16[1,256,1024]{2,1,0:T(8,128)(2,1)} copy(bf16[1,256,1024]{2,1,0:T(8,128)(2,1)} %get-tuple-element.30) | data formatting | bytes 1048576
  108.9 1.9 %copy.27 = bf16[1,256,1024]{2,1,0:T(8,128)(2,1)} copy(bf16[1,256,1024]{2,1,0:T(8,128)(2,1)} %get-tuple-element.31) | data formatting | bytes 1048576
  110.7 0.0 copy-done
  110.7 0.0 copy-start.1
  110.7 0.0 copy-start.2
  110.7 2.0 %copy.28 = bf16[1,2048,1024]{2,1,0:T(8,128)(2,1)} copy(bf16[1,2048,1024]{2,1,0:T(8,128)(2,1)S(1)} %copy-done) | data formatting | bytes 8388608
  112.7 0.0 copy-done.1
  112.7 0.6 copy.29
  113.3 0.0 copy-done.2
  113.3 0.6 copy.30
Async XLA Ops:
  103.1 7.7 %copy-start = (bf16[1,2048,1024]{2,1,0:T(8,128)(2,1)S(1)}, bf16[1,2048,1024]{2,1,0:T(8,128)(2,1)}, u32[]{:S(2)}) copy-start(bf16[1,2048,1024]{2,1,0:T(8,128)(2,1)} %get-tuple-element.32) | copy-start | bytes 12582916
  110.7 2.0 %copy-start.1 = (f32[1,2048]{1,0:T(1,128)S(1)}, f32[1,2048]{1,0:T(1,128)}, u32[]{:S(2)}) copy-start(f32[1,2048]{1,0:T(1,128)} %get-tuple-element.33) | copy-start | bytes 24580
  110.7 2.6 %copy-start.2 = (f32[1,1024]{1,0:T(1,128)S(1)}, f32[1,1024]{1,0:T(1,128)}, u32[]{:S(2)}) copy-start(f32[1,1024]{1,0:T(1,128)} %get-tuple-element.34) | copy-start | bytes 12292

commit v2 on v1

--- a/solution.py
+++ b/solution.py
@@ -46,7 +46,7 @@
     fwd_h, fwd_mem, saved_h, saved_mem, back_h, back_mem, weight, row_stat, col_stat, count, target,
     next_h, got_mem, prev_h, prev_mem, update, row_new, col_new,
     proj, sh, sm, xh, xm, tmp, left, fleft, qkv, probs, right, fmix,
-    th, tc, out, th_in, tc_in, out_in, inv, stats, grad, sums, acc, upd, send_h, send_m, send_y,
+    th, tc, out, th_in, tc_in, out_in, inv, stats, grad, sums, acc, send_h, send_m, send_y,
     local_sem, gather_s, gather_r, part_s, part_r, small_s, small_r, sec_s, sec_r,
 ):
     me = lax.axis_index("dp")
@@ -365,20 +365,13 @@
     sums[me, 0:1, :] = lax.rsqrt(row) * (jnp.sqrt(mean_row) / jnp.maximum(1.0, root))
     root_col = lax.rsqrt(col)
 
-    def update_copy(at, i):
-        return pltpu.make_async_copy(upd.at[at], update.at[0, at], local_sem.at[i])
-
     def update_body(i, carry):
         at = pl.ds(pl.multiple_of(i * step, step), step)
         factor = rows_to_lanes(sums[me, 0:1, at])[:, 0:1]
-        upd[at, :] = (grad[at, :] * factor * root_col).astype(BF16)
-        return carry
-
-    pieces = 4
-    size = full // pieces
-    for j in range(pieces):
-        lax.fori_loop(j * (size // step), (j + 1) * (size // step), update_body, 0)
-        update_copy(pl.ds(j * size, size), 8 + j).start()
+        update[0, at, :] = (grad[at, :] * factor * root_col).astype(BF16)
+        return carry
+
+    lax.fori_loop(0, full // step, update_body, 0)
 
     @pl.when(s == 0)
     def _():
@@ -414,8 +407,41 @@
             section_copy(1, t, send_h.at[t], prev_h.at[0, :, at], -1).wait_send()
             section_copy(2, t, send_m.at[t], prev_mem.at[0, :, at], -1).wait_send()
 
-    for j in range(pieces):
-        update_copy(pl.ds(j * size, size), 8 + j).wait()
+
+def finish(
+    next_h, got_mem, prev_h, prev_mem, update, row, col, count,
+    next_h_out, next_mem_out, prev_h_out, prev_mem_out, update_out, row_out, col_out, sem,
+):
+    before_dec = lax.axis_index("section") - 1 >= count[0]
+    pieces = 4
+    size = update.shape[1] // pieces
+    pairs = [
+        (update.at[0, pl.ds(j * size, size)], update_out.at[0, pl.ds(j * size, size)])
+        for j in range(pieces)
+    ]
+    pairs += [
+        (next_h, next_h_out),
+        (prev_h, prev_h_out),
+        (prev_mem, prev_mem_out),
+        (row, row_out),
+        (col, col_out),
+    ]
+    stores = [pltpu.make_async_copy(a, b, sem.at[i]) for i, (a, b) in enumerate(pairs)]
+    last = sem.at[len(pairs)]
+
+    @pl.when(before_dec)
+    def _():
+        pltpu.make_async_copy(got_mem, next_mem_out, last).start()
+
+    @pl.when(jnp.logical_not(before_dec))
+    def _():
+        pltpu.make_async_copy(next_h, next_mem_out, last).start()
+
+    for store in stores:
+        store.start()
+    pltpu.make_async_copy(next_h, next_mem_out, last).wait()
+    for store in stores:
+        store.wait()
 
 
 def on_device(
@@ -429,10 +455,12 @@
     tile = min(256, width)
     tiles = width // tile
     heads = cols // HD
-    hbm = pl.BlockSpec(memory_space=pl.ANY)
+    hbm = pl.BlockSpec(memory_space=pltpu.HBM)
+    anywhere = pl.BlockSpec(memory_space=pl.ANY)
     vmem = pl.BlockSpec(memory_space=pltpu.VMEM)
     smem = pl.BlockSpec(memory_space=pltpu.SMEM)
     act = jax.ShapeDtypeStruct((1, rows, width), BF16)
+    vact = pltpu.VMEM((1, rows, width), BF16)
     dma = pltpu.SemaphoreType.DMA
     parts = pltpu.VMEM((n, tiles, rows, tile), BF16)
     others = pltpu.VMEM((n - 1, tiles, rows, tile), BF16)
@@ -441,13 +469,13 @@
     next_h, got_mem, prev_h, prev_mem, update, row_new, col_new = pl.pallas_call(
         functools.partial(kernel, n, sections, rows, width, cols, tile),
         out_shape=(
-            act, act, act, act,
-            jax.ShapeDtypeStruct((1, full, cols), BF16),
-            jax.ShapeDtypeStruct((1, full), F32),
-            jax.ShapeDtypeStruct((1, cols), F32),
+            vact, vact, vact, vact,
+            pltpu.VMEM((1, full, cols), BF16),
+            pltpu.VMEM((1, full), F32),
+            pltpu.VMEM((1, cols), F32),
         ),
         in_specs=[hbm] * 7 + [vmem, vmem, smem, hbm],
-        out_specs=[hbm] * 5 + [vmem, vmem],
+        out_specs=[vmem] * 7,
         scratch_shapes=[
             pltpu.VMEM((full, cols), BF16),
             stored, stored, stored, stored,
@@ -464,24 +492,35 @@
             pltpu.VMEM((full, cols), F32),
             pltpu.VMEM((n, 8, full), F32),
             pltpu.VMEM((8, cols), F32),
-            pltpu.VMEM((full, cols), BF16),
             result, result, result,
-            dma((12,)),
+            dma((8,)),
             dma((5, n - 1)), dma((5, n - 1)),
             dma((3, n - 1, tiles)), dma((3, n - 1, tiles)),
             dma((2, n - 1)), dma((2, n - 1)),
             dma((4, tiles)), dma((4, tiles)),
         ],
         compiler_params=pltpu.CompilerParams(
-            collective_id=0, has_side_effects=True, vmem_limit_bytes=58 * MIB
+            collective_id=0, has_side_effects=True, vmem_limit_bytes=50 * MIB
         ),
     )(
         fwd_h, fwd_mem, saved_h, saved_mem, back_h, back_mem, weight, row_stat, col_stat,
         enc_count, target_embed,
     )
-    before_dec = lax.axis_index("section") - 1 >= enc_count[0]
-    next_mem = jnp.where(before_dec, got_mem, next_h)
-    return (next_h, next_mem, prev_h, prev_mem, update, row_new, col_new)
+    return tuple(
+        pl.pallas_call(
+            finish,
+            out_shape=(
+                act, act, act, act,
+                jax.ShapeDtypeStruct((1, full, cols), BF16),
+                jax.ShapeDtypeStruct((1, full), F32),
+                jax.ShapeDtypeStruct((1, cols), F32),
+            ),
+            in_specs=[anywhere] * 7 + [smem],
+            out_specs=[hbm] * 7,
+            scratch_shapes=[dma((10,))],
+            compiler_params=pltpu.CompilerParams(vmem_limit_bytes=MIB),
+        )(next_h, got_mem, prev_h, prev_mem, update, row_new, col_new, enc_count)
+    )
 
 
 def solution(mesh):

time: 114 us -> 105 us (0.921)
  local copies, waits for them, and re-layouts: 8.82 us -> 0 us
  other arithmetic: 2.05 us -> 0 us
    unnamed x12 -> x0, local copies, waits for them, and re-layouts: 8.82 us -> none
    pallas_call x0 -> x1, Pallas kernels: none -> 2.77 us  [on_device(): pl.pallas_call(finish, out_shape=(act, act, act, act, jax.ShapeDtypeStruc...]
    select_n x1 -> x0, other arithmetic: 2.05 us -> none  [on_device(): next_mem = jnp.where(before_dec, got_mem, next_h)]
    pallas_call x1, Pallas kernels: 102 us -> 100 us  [on_device(): pl.pallas_call(functools.partial(kernel, n, sections, rows, width, cols,...]
where the time goes in v2:
time: 105 us; the launch traced here: 104 us
  Pallas kernels  103 us (98%)
  between operations  1.29 us (1%)
    pallas_call x1, Pallas kernels, on_device(): pl.pallas_call(functools.partial(kernel, n, sections, rows, width, cols,...  100 us
    pallas_call x1, Pallas kernels, on_device(): pl.pallas_call(finish, out_shape=(act, act, act, act, jax.ShapeDtypeStruc...  2.77 us

profile of v2, /device:TPU:1, one launch (start us, length us, event | category | flops | bytes accessed | tf_op | source)
XLA Modules:
  0.0 104.3 jit_solution(13009078163636307496)
XLA Ops:
  1.3 100.2 %shard_map.162 = (bf16[1,256,1024]{2,1,0:T(8,128)(2,1)S(1)}, bf16[1,256,1024]{2,1,0:T(8,128)(2,1)S(1)}, bf16[1,256,1024]{2,1,0:T(8,128)(2,1)S(1)}, bf16[1,256,10...) custom-call(bf16[1,256,1024]{2,1,0:T(8,128)(2,1)} %fwd_h.1, ...), custom_call_target="tpu_custom_call" | custom-call | tf_op jit(solution)/shard_map/pallas_call | solution.py:469
  101.5 2.8 %shard_map.163 = (bf16[1,256,1024]{2,1,0:T(8,128)(2,1)}, bf16[1,256,1024]{2,1,0:T(8,128)(2,1)}, bf16[1,256,1024]{2,1,0:T(8,128)(2,1)}, bf16[1,256,1024]{2,1,0:T(...) custom-call(bf16[1,256,1024]{2,1,0:T(8,128)(2,1)S(1)} %get-tuple-element.14.next_h, ...), custom_call_target="tpu_custom_call" | custom-call | tf_op jit(solution)/shard_map/pallas_call | solution.py:510

commit v3 on v2

--- a/solution.py
+++ b/solution.py
@@ -34,7 +34,7 @@
     rows = first.shape[0]
     lane = lax.broadcasted_iota(jnp.int32, (rows, 128), 1)
     both = jnp.where(lane == 0, first, second)
-    return jnp.transpose(both)[0:8]
+    return jnp.transpose(both)[0:2]
 
 
 def rows_to_lanes(row):
@@ -47,7 +47,8 @@
     next_h, got_mem, prev_h, prev_mem, update, row_new, col_new,
     proj, sh, sm, xh, xm, tmp, left, fleft, qkv, probs, right, fmix,
     th, tc, out, th_in, tc_in, out_in, inv, stats, grad, sums, acc, send_h, send_m, send_y,
-    local_sem, gather_s, gather_r, part_s, part_r, small_s, small_r, sec_s, sec_r,
+    hop1, hop2, local_sem, gather_s, gather_r, part_s, part_r, small_s, small_r, sec_s, sec_r,
+    hop_s, hop_r,
 ):
     me = lax.axis_index("dp")
     s = lax.axis_index("section")
@@ -60,6 +61,27 @@
     is_first = (s == first_dec).astype(jnp.int32)
     is_last_enc = (s == first_dec - 1).astype(jnp.int32)
     own_tmp = [tmp.at[i] for i in range(4)]
+    relayed = n == 2
+    quarter = sections // 4
+    cut = rows // 2 if relayed else rows
+    carries = s < quarter
+    base = lax.rem(s, quarter)
+    hop_slot = jnp.maximum(s // quarter - 1, 0)
+
+    def when_carrying(f):
+        if relayed:
+            pl.when(carries)(f)
+
+    def when_carried(f):
+        if relayed:
+            pl.when(jnp.logical_not(carries))(f)
+
+    def unless_carrying(f):
+        if relayed:
+            pl.when(jnp.logical_not(carries))(f)
+        else:
+            f()
+
 
     def peer(k):
         return lax.rem(me + k, n)
@@ -93,8 +115,19 @@
     def _():
         pl.semaphore_signal(barrier, 1, device_id={"section": s + 1}, device_id_type=MESH)
 
+    @when_carrying
+    def _():
+        for j in range(3):
+            far = {"section": s + quarter * (j + 1)}
+            pl.semaphore_signal(barrier, 1, device_id=far, device_id_type=MESH)
+
+    @when_carried
+    def _():
+        pl.semaphore_signal(barrier, 1, device_id={"section": base}, device_id_type=MESH)
+
     ends = (s > 0).astype(jnp.int32) + (s < sections - 1).astype(jnp.int32)
-    pl.semaphore_wait(barrier, n - 1 + ends)
+    hops = jnp.where(carries, 3, 1) if relayed else 0
+    pl.semaphore_wait(barrier, n - 1 + ends + hops)
 
     def to_peer(src, dst, send, recv, k):
         return pltpu.make_async_remote_copy(
@@ -115,7 +148,37 @@
         return left.at[p, pl.ds(r2, rows)]
 
     gather_start(0, saved_h.at[0], lambda p: sh.at[p])
-    gather_start(1, saved_mem.at[0], lambda p: sm.at[p])
+
+    def hop1_copy(j):
+        return pltpu.make_async_remote_copy(
+            fwd_mem.at[0, pl.ds(rows - cut, cut)], hop1.at[j], hop_s.at[0, 0], hop_r.at[0, j],
+            device_id={"section": base}, device_id_type=MESH,
+        )
+
+    def hop2_copy(j):
+        return to_peer(hop1.at[j], hop2.at[j], hop_s.at[1, j], hop_r.at[1, j], 1)
+
+    def hop3_copy(j):
+        return pltpu.make_async_remote_copy(
+            hop2.at[j], xm.at[source(1), pl.ds(rows - cut, cut)], hop_s.at[2, j], hop_r.at[2, 0],
+            device_id={"section": base + quarter * (j + 1)}, device_id_type=MESH,
+        )
+
+    @when_carried
+    def _():
+        hop1_copy(hop_slot).start()
+
+    def sm_slot(p):
+        return sm.at[p]
+
+    def xm_slot(p):
+        return xm.at[p, pl.ds(0, cut)]
+
+    xm_own = fwd_mem.at[0, pl.ds(0, cut)]
+
+    @unless_carrying
+    def _():
+        gather_start(1, saved_mem.at[0], sm_slot)
 
     def section_copy(i, t, src, dst, by):
         return pltpu.make_async_remote_copy(
@@ -180,8 +243,19 @@
     loads[4].wait()
     loads[5].wait()
     gather_wait(0, saved_h.at[0], lambda p: sh.at[p])
+
+    @when_carrying
+    def _():
+        for j in range(3):
+            hop1_copy(j).wait_recv()
+            hop2_copy(j).start()
+
     gather_start(2, g_slot(me), g_slot)
-    gather_wait(1, saved_mem.at[0], lambda p: sm.at[p])
+
+    @unless_carrying
+    def _():
+        gather_wait(1, saved_mem.at[0], sm_slot)
+
     gather_start(3, xh.at[me], lambda p: xh.at[p])
     normalize(sh, sm, left, True)
     loads[6].wait()
@@ -198,8 +272,18 @@
 
     lax.fori_loop(0, heads, attend_body, 0)
 
+    @when_carrying
+    def _():
+        for j in range(3):
+            hop2_copy(j).wait_recv()
+            hop3_copy(j).start()
+
     gather_wait(2, g_slot(me), g_slot)
-    gather_start(4, fwd_mem.at[0], lambda p: xm.at[p])
+
+    @unless_carrying
+    def _():
+        gather_start(4, xm_own, xm_slot)
+
 
     def back_body(h, carry):
         stat_q, stat_k = carry
@@ -245,7 +329,11 @@
         for t in range(tiles):
             terms(peer(k), t, th.at[k - 1, t], tc.at[k - 1, t])
             part_copy(0, k, t, th, th_in).start()
-            part_copy(1, k, t, tc, tc_in).start()
+
+            @unless_carrying
+            def _():
+                part_copy(1, k, t, tc, tc_in).start()
+
 
     def own_terms(t, carry):
         terms(me, t, th_in.at[0, t], tc_in.at[0, t])
@@ -255,7 +343,15 @@
 
     loads[7].wait()
     gather_wait(3, xh.at[me], lambda p: xh.at[p])
-    gather_wait(4, fwd_mem.at[0], lambda p: xm.at[p])
+
+    @unless_carrying
+    def _():
+        gather_wait(4, xm_own, xm_slot)
+
+    @when_carried
+    def _():
+        hop3_copy(hop_slot).wait_recv()
+
     normalize(xh, xm, fleft, False)
 
     def forward_body(h, carry):
@@ -328,7 +424,11 @@
     for t in range(tiles):
         for k in range(1, n):
             part_copy(0, k, t, th, th_in).wait()
-            part_copy(1, k, t, tc, tc_in).wait()
+
+            @unless_carrying
+            def _():
+                part_copy(1, k, t, tc, tc_in).wait()
+
         share_h = sum(th_in[k, t].astype(F32) for k in range(n))
         share_c = sum(tc_in[k, t].astype(F32) for k in range(n))
         at = tile_cols(t)
@@ -372,6 +472,16 @@
         return carry
 
     lax.fori_loop(0, full // step, update_body, 0)
+
+    @when_carried
+    def _():
+        hop1_copy(hop_slot).wait_send()
+
+    @when_carrying
+    def _():
+        for j in range(3):
+            hop2_copy(j).wait_send()
+            hop3_copy(j).wait_send()
 
     @pl.when(s == 0)
     def _():
@@ -488,16 +598,19 @@
             pltpu.VMEM((rows, cols), BF16),
             others, others, others, parts, parts, parts,
             pltpu.VMEM((2, rows, 128), F32),
-            pltpu.VMEM((n, 8, rows), F32),
+            pltpu.VMEM((n, 2, rows), F32),
             pltpu.VMEM((full, cols), F32),
-            pltpu.VMEM((n, 8, full), F32),
+            pltpu.VMEM((n, 2, full), F32),
             pltpu.VMEM((8, cols), F32),
             result, result, result,
+            pltpu.VMEM((3, rows // 2, width), BF16),
+            pltpu.VMEM((3, rows // 2, width), BF16),
             dma((8,)),
             dma((5, n - 1)), dma((5, n - 1)),
             dma((3, n - 1, tiles)), dma((3, n - 1, tiles)),
             dma((2, n - 1)), dma((2, n - 1)),
             dma((4, tiles)), dma((4, tiles)),
+            dma((3, 3)), dma((3, 3)),
         ],
         compiler_params=pltpu.CompilerParams(
             collective_id=0, has_side_effects=True, vmem_limit_bytes=50 * MIB

time: 105 us -> 102 us (0.971)
  Pallas kernels: 103 us -> 100 us
    pallas_call x1, Pallas kernels: 100 us -> 97.3 us  [on_device(): pl.pallas_call(functools.partial(kernel, n, sections, rows, width, cols,...]
where the time goes in v3:
time: 102 us; the launch traced here: 101 us
  Pallas kernels  100 us (98%)
  between operations  1.29 us (1%)
    pallas_call x1, Pallas kernels, on_device(): pl.pallas_call(functools.partial(kernel, n, sections, rows, width, cols,...  97.3 us
    pallas_call x1, Pallas kernels, on_device(): pl.pallas_call(finish, out_shape=(act, act, act, act, jax.ShapeDtypeStruc...  2.77 us

profile of v3, /device:TPU:1, one launch (start us, length us, event | category | flops | bytes accessed | tf_op | source)
XLA Modules:
  0.0 101.4 jit_solution(15607850035717414587)
XLA Ops:
  1.3 97.3 %shard_map.162 = (bf16[1,256,1024]{2,1,0:T(8,128)(2,1)S(1)}, bf16[1,256,1024]{2,1,0:T(8,128)(2,1)S(1)}, bf16[1,256,1024]{2,1,0:T(8,128)(2,1)S(1)}, bf16[1,256,10...) custom-call(bf16[1,256,1024]{2,1,0:T(8,128)(2,1)} %fwd_h.1, ...), custom_call_target="tpu_custom_call" | custom-call | tf_op jit(solution)/shard_map/pallas_call | solution.py:579
  98.6 2.8 %shard_map.163 = (bf16[1,256,1024]{2,1,0:T(8,128)(2,1)}, bf16[1,256,1024]{2,1,0:T(8,128)(2,1)}, bf16[1,256,1024]{2,1,0:T(8,128)(2,1)}, bf16[1,256,1024]{2,1,0:T(...) custom-call(bf16[1,256,1024]{2,1,0:T(8,128)(2,1)S(1)} %get-tuple-element.14.next_h, ...), custom_call_target="tpu_custom_call" | custom-call | tf_op jit(solution)/shard_map/pallas_call | solution.py:623
